TPU v7x, 128 devices: a whole 4x4x4 slice. The times are simulated.
128 devices in a mesh: seq: 16 (over x_lo, y, core), head: 8 (over z, x_hi).
Axes of the slice: x: 4 (x_hi: 2, x_lo: 2; x = x_hi * 2 + x_lo), y: 4, z: 4, core: 2. Of those that a mesh axis runs over, the one named last changes fastest.
Arguments:
- out_grad: bfloat16 [16384, 6144], P(('seq', 'head')), may hold values from -96 to 96
- expert_rows: bfloat16 [8, 8192, 6144], P('head', 'seq'), may hold values from -96 to 96
- expert_ids: int32 [16384, 2], P(('seq', 'head')), may hold values from 0 to 7, all different within a row; in each aligned block of 128 rows (0 to 127, 128 to 255, ...) at most 64 rows name the same one
- gates: float32 [16384, 2], P(('seq', 'head')), may hold values from 0.1 to 0.9
- out_proj: bfloat16 [3072, 6144], P('head'), may hold values from -0.078125 to 0.078125
- attention_output: bfloat16 [24, 16384, 128], P('head', 'seq'), may hold values from -0.0029296875 to 0.0029296875
- saved_queries: bfloat16 [24, 16384, 128], P('head', 'seq'), may hold values from -1.6953125 to 1.6953125
- saved_keys: bfloat16 [8, 16384, 128], P('head', 'seq'), may hold values from -1.6953125 to 1.6953125
- saved_values: bfloat16 [8, 16384, 128], P('head', 'seq'), may hold values from -6 to 6
- softmax_normalizer: float32 [24, 16384], P('head', 'seq'), may hold values from 8 to 9.5
Outputs:
- grad_query: bfloat16 [16384, 3072], P(('seq', 'head'))
- key_gradient_rows: bfloat16 [16384, 1024], P(('seq', 'head'))
- value_gradient_rows: bfloat16 [16384, 1024], P(('seq', 'head'))
- grad_proj: bfloat16 [3072, 6144], P('head')
Inputs may be any that keep to these rules, and one draw needn't show every extreme that they name: `expert_ids`: each row names 2 different experts. In each aligned block of 128 rows (the tokens of one device) no expert is named more than 64 times, a bound that some block reaches.
All inputs are finite; a program needn't handle non-finite values.
Results may differ from a plain program's by a relative error of at most 0.0065.
Values may be sent and summed in bfloat16 or wider, within the bound.
A program may use at most 128 MiB of HBM per device.

v0:
```python
import math
import jax
import jax.numpy as jnp
from jax import lax
from jax.sharding import PartitionSpec as P

WIN = 4096


def shifted(block, axis, distance):
    devices = range(lax.axis_size(axis))
    route = [(i - distance, i) for i in devices if i - distance in devices]
    return lax.ppermute(block, axis, route)


def routed_rows(returned, expert_ids):
    experts = returned.shape[0]
    capacity = returned.shape[1]
    model_width = returned.shape[2]
    pair_ids = expert_ids.reshape(-1)
    onehot = (pair_ids[:, None] == jnp.arange(experts, dtype=jnp.int32)[None, :]).astype(jnp.int32)
    before = jnp.cumsum(onehot, axis=0) - onehot
    slot_rank = jnp.sum(before * onehot, axis=1)
    flat_index = pair_ids * capacity + slot_rank
    row_table = returned.reshape(experts * capacity, model_width)
    picked = jnp.take(row_table, flat_index, axis=0)
    return picked.reshape(expert_ids.shape[0], expert_ids.shape[1], model_width)


def local(
    out_grad,
    expert_rows,
    expert_ids,
    gates,
    out_proj,
    attention_output,
    saved_queries,
    saved_keys,
    saved_values,
    softmax_normalizer,
):
    heads_dev, seq_dev, head_dim = saved_queries.shape
    kv_dev = saved_keys.shape[0]
    group_size = heads_dev // kv_dev
    model_width = out_grad.shape[1]
    returned = lax.all_to_all(expert_rows, "head", split_axis=1, concat_axis=0, tiled=True)
    picked = routed_rows(returned, expert_ids)
    summed = out_grad.astype(jnp.float32)
    summed = summed + gates[:, 0:1] * picked[:, 0].astype(jnp.float32)
    summed = summed + gates[:, 1:2] * picked[:, 1].astype(jnp.float32)
    hidden = summed.astype(jnp.bfloat16)
    piece = lax.all_gather(hidden, "head", axis=0, tiled=True)
    fresh_rows = lax.dot_general(
        piece, out_proj, (((1,), (1,)), ((), ())), preferred_element_type=jnp.float32
    ).astype(jnp.bfloat16)
    partial_value = lax.dot_general(
        attention_output, piece, (((1,), (0,)), ((), ())), preferred_element_type=jnp.float32
    )
    grad_out, partial_value = (fresh_rows, partial_value)
    summed_proj = lax.psum(partial_value, "seq")
    grad_proj = summed_proj.astype(jnp.bfloat16).reshape(heads_dev * head_dim, model_width)
    head_gradients = jnp.transpose(grad_out.reshape(seq_dev, heads_dev, head_dim), (1, 0, 2))
    row_delta = jnp.sum(
        head_gradients.astype(jnp.float32) * attention_output.astype(jnp.float32), axis=2
    )
    window = WIN
    span_count = (window + seq_dev - 1) // seq_dev
    offset = span_count * seq_dev
    kv_pair = jnp.stack([saved_keys, saved_values], axis=0)
    earlier = []
    for distance in range(span_count, 0, -1):
        earlier.append(shifted(kv_pair, "seq", distance))
    extended = jnp.concatenate(earlier + [kv_pair], axis=2)
    block_rows = min(512, seq_dev)
    key_span = window + block_rows
    score_scale = 1.0 / math.sqrt(head_dim)
    seq_pos = lax.axis_index("seq")
    rows_iota = lax.broadcasted_iota(jnp.int32, (block_rows, key_span), 0)
    cols_iota = lax.broadcasted_iota(jnp.int32, (block_rows, key_span), 1)
    in_band = (cols_iota >= rows_iota + 1) & (cols_iota <= rows_iota + window)
    ext_len = offset + seq_dev

    def block_step(index, carry):
        dk_ext, dv_ext, dq_all = carry
        first_row = index * block_rows
        key_start = first_row + (offset - window)
        usable = in_band & (cols_iota + key_start >= offset - seq_pos * seq_dev)
        key_blk = lax.dynamic_slice_in_dim(extended[0, 0], key_start, key_span, 0)
        value_blk = lax.dynamic_slice_in_dim(extended[1, 0], key_start, key_span, 0)
        dk_blk = jnp.zeros((key_span, head_dim), jnp.float32)
        dv_blk = jnp.zeros((key_span, head_dim), jnp.float32)
        for q_head in range(0, group_size):
            query_blk = lax.dynamic_slice_in_dim(saved_queries[q_head], first_row, block_rows, 0)
            grad_blk = lax.dynamic_slice(
                grad_out, (first_row, q_head * head_dim), (block_rows, head_dim)
            )
            lse_blk = lax.dynamic_slice_in_dim(softmax_normalizer[q_head], first_row, block_rows, 0)
            delta_blk = lax.dynamic_slice_in_dim(row_delta[q_head], first_row, block_rows, 0)
            scores = (
                lax.dot_general(
                    query_blk, key_blk, (((1,), (1,)), ((), ())), preferred_element_type=jnp.float32
                )
                * score_scale
            )
            probability = jnp.where(usable, jnp.exp(scores - lse_blk[:, None]), 0.0)
            grad_prob = lax.dot_general(
                grad_blk, value_blk, (((1,), (1,)), ((), ())), preferred_element_type=jnp.float32
            )
            grad_score = probability * (grad_prob - delta_blk[:, None])
            prob_half = probability.astype(jnp.bfloat16)
            score_half = grad_score.astype(jnp.bfloat16)
            dv_blk = dv_blk + lax.dot_general(
                prob_half, grad_blk, (((0,), (0,)), ((), ())), preferred_element_type=jnp.float32
            )
            dk_blk = dk_blk + score_scale * lax.dot_general(
                score_half, query_blk, (((0,), (0,)), ((), ())), preferred_element_type=jnp.float32
            )
            dq_blk = score_scale * jnp.dot(score_half, key_blk, preferred_element_type=jnp.float32)
            dq_all = lax.dynamic_update_slice(dq_all, dq_blk, (first_row, q_head * head_dim))
        old_key = lax.dynamic_slice(dk_ext, (0, key_start, 0), (1, key_span, head_dim))
        dk_ext = lax.dynamic_update_slice(dk_ext, old_key + dk_blk[None], (0, key_start, 0))
        old_value = lax.dynamic_slice(dv_ext, (0, key_start, 0), (1, key_span, head_dim))
        dv_ext = lax.dynamic_update_slice(dv_ext, old_value + dv_blk[None], (0, key_start, 0))
        return (dk_ext, dv_ext, dq_all)

    loop_carry = (
        jnp.zeros((kv_dev, ext_len, head_dim), jnp.float32),
        jnp.zeros((kv_dev, ext_len, head_dim), jnp.float32),
        jnp.zeros((seq_dev, heads_dev * head_dim), jnp.float32),
    )
    dk_ext, dv_ext, dq_all = lax.fori_loop(0, seq_dev // block_rows, block_step, loop_carry)
    grads_ext = jnp.stack([dk_ext, dv_ext], axis=0)
    total_kv = grads_ext[:, :, offset:, :]
    for distance in range(1, span_count + 1):
        far_part = grads_ext[
            :, :, offset - distance * seq_dev : offset - (distance - 1) * seq_dev, :
        ]
        total_kv = total_kv + shifted(far_part, "seq", -distance)
    kv_half = total_kv.astype(jnp.bfloat16)
    dk_cols = jnp.transpose(kv_half[0], (1, 0, 2)).reshape(seq_dev, kv_dev * head_dim)
    dv_cols = jnp.transpose(kv_half[1], (1, 0, 2)).reshape(seq_dev, kv_dev * head_dim)
    dq_cols = dq_all.astype(jnp.bfloat16)
    grad_query, key_gradient_rows, value_gradient_rows = (
        lax.all_to_all(dq_cols, "head", split_axis=0, concat_axis=1, tiled=True),
        lax.all_to_all(dk_cols, "head", split_axis=0, concat_axis=1, tiled=True),
        lax.all_to_all(dv_cols, "head", split_axis=0, concat_axis=1, tiled=True),
    )
    return (grad_query, key_gradient_rows, value_gradient_rows, grad_proj)


def solution(mesh):
    in_specs = (
        P(("seq", "head"), None),
        P("head", "seq", None),
        P(("seq", "head"), None),
        P(("seq", "head"), None),
        P("head", None),
        P("head", "seq", None),
        P("head", "seq", None),
        P("head", "seq", None),
        P("head", "seq", None),
        P("head", "seq"),
    )
    out_specs = (
        P(("seq", "head"), None),
        P(("seq", "head"), None),
        P(("seq", "head"), None),
        P("head", None),
    )
    return jax.shard_map(local, mesh=mesh, in_specs=in_specs, out_specs=out_specs, check_vma=False)
```

profile of v0, /device:TPU:6, one launch (start us, length us, event | category | flops | bytes accessed | tf_op | source)
XLA Modules:
  0.0 762.1 jit_solution(4666393536093147817)
XLA Ops:
  7.2 12.2 %copy.78 = bf16[1,512,6144]{2,0,1:T(2,128)(2,1)} copy(bf16[1,512,6144]{2,1,0:T(8,128)(2,1)} %param.13) | data formatting | bytes 12582912 | tf_op args[1]
  19.9 38.9 %reduce.2 = bf16[512,6144]{1,0:T(8,128)(2,1)} reduce(bf16[512,1,6144]{2,1,0:T(2,128)(2,1)} %bitcast.199, bf16[]{:T(256)} %broadcast.111), dimensions={1}, to_apply=%bitcast.134.reduce_sub_computation | reduce | bytes 12582914
  58.8 9.4 %reshape.158 = bf16[8,2,196608]{2,1,0:T(2,128)(2,1)} reshape(bf16[512,6144]{1,0:T(8,128)(2,1)} %reduce.2) | data formatting | bytes 12582912
  68.2 8.4 %all-to-all-start = ((bf16[8,2,196608]{2,1,0:T(2,128)(2,1)}), bf16[8,2,196608]{2,1,0:T(2,128)(2,1)}, u32[]{:S(2)}, u32[]{:S(2)}) async-start(bf16[8,2,196608]{2,1,0:T(2,128)(2,1)} %reshape.158), calls=%async_computation | async-start | bytes 12582912 | tf_op jit(solution)/shard_map/all_to_all | solution.py:46
  80.3 67.1 %all-to-all-done = bf16[8,2,196608]{2,1,0:T(2,128)(2,1)} async-done(((bf16[8,2,196608]{2,1,0:T(2,128)(2,1)}), bf16[8,2,196608]{2,1,0:T(2,128)(2,1)}, u32[]{:S(2)}, u32[]{:S(2)}) %all-to-all-start) | async-done | bytes 6291488 | tf_op jit(solution)/shard_map/all_to_all | solution.py:46
  147.4 11.0 %reshape.159 = bf16[512,1,6144]{2,1,0:T(2,128)(2,1)} reshape(bf16[8,2,196608]{2,1,0:T(2,128)(2,1)} %all-to-all-done) | data formatting | bytes 12582912
  158.4 11.0 %copy.77 = bf16[1,512,6144]{2,1,0:T(8,128)(2,1)} copy(bf16[1,512,6144]{2,0,1:T(2,128)(2,1)} %bitcast.198) | data formatting | bytes 12582912
  169.4 9.1 %gather_fusion = bf16[256,6144]{1,0:T(8,128)(2,1)S(1)} fusion(bf16[512,6144]{1,0:T(8,128)(2,1)} %bitcast.197, s32[1024]{0:T(1024)S(1)} %pad_clamp_fusion), kind=kCustom, calls=%fused_computation | custom fusion | bytes 6292480 | tf_op jit(solution)/shard_map/jit(_take)/gather | solution.py:26
  181.7 7.7 %copy.64 = bf16[128,2,6144]{0,2,1:T(8,128)(2,1)S(1)} copy(bf16[128,2,6144]{2,1,0:T(2,128)(2,1)} %gather.7) | data formatting | bytes 6291456 | tf_op jit(solution)/shard_map/jit(_take)/gather | solution.py:26
  193.7 5.1 collective-permute-start
  205.2 13.0 %collective-permute-done = bf16[2,1,1024,128]{3,2,1,0:T(8,128)(2,1)} collective-permute-done((bf16[2,1,1024,128]{3,2,1,0:T(8,128)(2,1)}, bf16[2,1,1024,128]{3,2,1,0:T(8,128)(2,1)}, u32[]{:S(2)}, u32[]{:S(2)}) %collective-permute-start) | collective-permute-done | bytes 524320 | tf_op jit(solution)/shard_map/ppermute | solution.py:13
  219.3 8.6 %collective-permute-done.1 = bf16[2,1,1024,128]{3,2,1,0:T(8,128)(2,1)} collective-permute-done((bf16[2,1,1024,128]{3,2,1,0:T(8,128)(2,1)}, bf16[2,1,1024,128]{3,2,1,0:T(8,128)(2,1)}, u32[]{:S(2)}, u32[]{:S(2)}) %collective-permute-start.1) | collective-permute-done | bytes 524320 | tf_op jit(solution)/shard_map/ppermute | solution.py:13
  229.0 24.2 %collective-permute-done.2 = bf16[2,1,1024,128]{3,2,1,0:T(8,128)(2,1)} collective-permute-done((bf16[2,1,1024,128]{3,2,1,0:T(8,128)(2,1)}, bf16[2,1,1024,128]{3,2,1,0:T(8,128)(2,1)}, u32[]{:S(2)}, u32[]{:S(2)}) %collective-permute-start.2) | collective-permute-done | bytes 524320 | tf_op jit(solution)/shard_map/ppermute | solution.py:13
  257.6 103.3 %all-gather.2.cloned.1.call-done = bf16[1024,6144]{0,1:T(8,128)(2,1)} async-done(((bf16[128,6144]{0,1:T(8,128)(2,1)}), bf16[1024,6144]{0,1:T(8,128)(2,1)}) %all-gather.2.cloned.1.call-update) | async-done | bytes 12582928 | tf_op jit(solution)/shard_map/all_gather | solution.py:52
  360.9 10.1 %convolution_convert_fusion = bf16[1024,384]{0,1:T(8,128)(2,1)} fusion(bf16[384,6144]{1,0:T(8,128)(2,1)} %param.16, bf16[1024,6144]{0,1:T(8,128)(2,1)} %all-gather.2.cloned.1.call-done), kind=kOutput, calls=%fused_computation.121 | convolution fusion | flops 4832231424 | bytes 18087936 | tf_op jit(solution)/shard_map/dot_general | solution.py:53
  381.5 99.3 %while.20 = (s32[]{:T(128)}, f32[1,5120,128]{2,1,0:T(8,128)}, f32[1,5120,128]{2,1,0:T(8,128)}, bf16[1024,384]{1,0:T(8,128)(2,1)}, s32[]{:T(128)}, /*index=5*/bf1...) while((s32[]{:T(128)}, f32[1,5120,128]{2,1,0:T(8,128)}, ...), condition=%wide.region_5.6_spmd.clone, body=%wide.region_4.5_spmd.clone.sunk | while | flops 9156034560 | bytes 252151056 | solution.py:131
  399.5 5.2 exponential_select_fusion.6
  409.4 4.9 fusion.204
  426.4 4.7 fusion.202
  448.9 5.2 exponential_select_fusion.6
  458.9 4.9 fusion.204
  495.3 7.1 all-to-all-start.1
  502.4 23.6 %collective-permute-done.4 = f32[2,1,1024,128]{3,2,1,0:T(8,128)S(1)} collective-permute-done((f32[2,1,1024,128]{3,2,1,0:T(8,128)}, f32[2,1,1024,128]{3,2,1,0:T(8,128)S(1)}, u32[]{:S(2)}, u32[]{:S(2)}) %collective-permute-start.4) | collective-permute-done | bytes 1048608 | tf_op jit(solution)/shard_map/ppermute | solution.py:13
  525.9 30.3 %collective-permute-done.5 = f32[2,1,1024,128]{3,2,1,0:T(8,128)} collective-permute-done((f32[2,1,1024,128]{3,2,1,0:T(8,128)}, f32[2,1,1024,128]{3,2,1,0:T(8,128)}, u32[]{:S(2)}, u32[]{:S(2)}) %collective-permute-start.5) | collective-permute-done | bytes 1048608 | tf_op jit(solution)/shard_map/ppermute | solution.py:13
  556.2 22.5 %collective-permute-done.7 = f32[2,1,1024,128]{3,2,1,0:T(8,128)} collective-permute-done((f32[2,1,1024,128]{3,2,1,0:T(8,128)}, f32[2,1,1024,128]{3,2,1,0:T(8,128)}, u32[]{:S(2)}, u32[]{:S(2)}) %collective-permute-start.7) | collective-permute-done | bytes 1048608 | tf_op jit(solution)/shard_map/ppermute | solution.py:13
  578.7 17.8 %collective-permute-done.6 = f32[2,1,1024,128]{3,2,1,0:T(8,128)} collective-permute-done((f32[2,1,1024,128]{3,2,1,0:T(8,128)S(1)}, f32[2,1,1024,128]{3,2,1,0:T(8,128)}, u32[]{:S(2)}, u32[]{:S(2)}) %collective-permute-start.6) | collective-permute-done | bytes 1048608 | tf_op jit(solution)/shard_map/ppermute | solution.py:13
  599.8 6.4 all-to-all-done.1
  606.1 6.0 all-to-all-start.2
  612.2 11.8 %fusion.95 = f32[3,128,6144]{1,2,0:T(8,128)} fusion(bf16[3,1024,128]{2,1,0:T(8,128)(2,1)S(1)} %copy-done.16, bf16[1024,6144]{0,1:T(8,128)(2,1)} %all-gather.2.cloned.1.call-done), kind=kOutput, calls=%fused_computation.101 | convolution fusion | flops 4831838208 | bytes 22806528 | tf_op jit(solution)/shard_map/dot_general | solution.py:56
  624.0 7.2 all-to-all-start.3
  631.2 113.4 %all-reduce.1 = bf16[3,128,6144]{1,2,0:T(8,128)(2,1)} all-reduce(f32[3,128,6144]{1,2,0:T(8,128)} %fusion.95), channel_id=1, replica_groups=mesh['seq'=16,'head'=8] {'seq'}, use_global_device_ids=true, to_apply=%region_6.7 | all-reduce | flops 2359296 | bytes 14155776 | tf_op jit(solution)/shard_map/psum | solution.py:60
  744.6 6.6 copy.70
  (184 shorter events, 130.0 us)
Async XLA Ops:
  68.2 8.4 %copy-start.18 = (s32[128,2]{0,1:T(2,128)S(1)}, s32[128,2]{0,1:T(2,128)}, u32[]{:S(2)}) copy-start(s32[128,2]{0,1:T(2,128)} %param.14) | copy-start | bytes 3076
  68.2 10.5 %copy-start.13 = (bf16[128,6144]{1,0:T(8,128)(2,1)S(1)}, bf16[128,6144]{1,0:T(8,128)(2,1)}, u32[]{:S(2)}) copy-start(bf16[128,6144]{1,0:T(8,128)(2,1)} %param.12) | copy-start | bytes 4718596
  68.2 79.2 %all-to-all-start = ((bf16[8,2,196608]{2,1,0:T(2,128)(2,1)}), bf16[8,2,196608]{2,1,0:T(2,128)(2,1)}, u32[]{:S(2)}, u32[]{:S(2)}) async-start(bf16[8,2,196608]{2,1,0:T(2,128)(2,1)} %reshape.158), calls=%async_computation | async-start | bytes 12582912 | tf_op jit(solution)/shard_map/all_to_all | solution.py:46
  76.6 284.3 %all-gather.2.cloned.1.call-start = ((), (), s32[]{:S(2)}) async-start(), calls=%async_computation.4 | async-start | bytes 14155776 | tf_op jit(solution)/shard_map/all_gather | solution.py:52
  193.7 24.5 %collective-permute-start = (bf16[2,1,1024,128]{3,2,1,0:T(8,128)(2,1)}, bf16[2,1,1024,128]{3,2,1,0:T(8,128)(2,1)}, u32[]{:S(2)}, u32[]{:S(2)}) collective-permute-start(bf16[2,1,1024,128]{3,2,1,0:T(8,128)(2,1)} %pad_maximum_fusion.1), channel_id=1, source_target_pairs={{0,32},{8,40},{16,48},{24,56},{32,64},{40,72},{48,80},{56,88},{64,... | collective-permute-start | bytes 1572872 | tf_op jit(solution)/shard_map/ppermute | solution.py:13
  198.8 29.1 %collective-permute-start.1 = (bf16[2,1,1024,128]{3,2,1,0:T(8,128)(2,1)}, bf16[2,1,1024,128]{3,2,1,0:T(8,128)(2,1)}, u32[]{:S(2)}, u32[]{:S(2)}) collective-permute-start(bf16[2,1,1024,128]{3,2,1,0:T(8,128)(2,1)} %pad_maximum_fusion.1), channel_id=1, source_target_pairs={{0,24},{8,32},{16,40},{24,48},{32,56},{40,64},{48,72},{56,80},{64,... | collective-permute-start | bytes 1572872 | tf_op jit(solution)/shard_map/ppermute | solution.py:13
  200.7 52.5 %collective-permute-start.2 = (bf16[2,1,1024,128]{3,2,1,0:T(8,128)(2,1)}, bf16[2,1,1024,128]{3,2,1,0:T(8,128)(2,1)}, u32[]{:S(2)}, u32[]{:S(2)}) collective-permute-start(bf16[2,1,1024,128]{3,2,1,0:T(8,128)(2,1)} %pad_maximum_fusion.1), channel_id=1, source_target_pairs={{0,16},{8,24},{16,32},{24,40},{32,48},{40,56},{48,64},{56,72},{64,... | collective-permute-start | bytes 1572872 | tf_op jit(solution)/shard_map/ppermute | solution.py:13
  203.3 53.1 %collective-permute-start.3 = (bf16[2,1,1024,128]{3,2,1,0:T(8,128)(2,1)}, bf16[2,1,1024,128]{3,2,1,0:T(8,128)(2,1)}, u32[]{:S(2)}, u32[]{:S(2)}) collective-permute-start(bf16[2,1,1024,128]{3,2,1,0:T(8,128)(2,1)} %pad_maximum_fusion.1), channel_id=1, source_target_pairs={{0,8},{8,16},{16,24},{24,32},{32,40},{40,48},{48,56},{56,64},{64,7... | collective-permute-start | bytes 1572872 | tf_op jit(solution)/shard_map/ppermute | solution.py:13
  381.7 14.1 %copy-start.5 = (bf16[1024,384]{1,0:T(8,128)(2,1)}, bf16[1024,384]{1,0:T(8,128)(2,1)S(1)}, u32[]{:S(2)}) copy-start(bf16[1024,384]{1,0:T(8,128)(2,1)S(1)} %get-tuple-element.567) | copy-start | bytes 2359300 | tf_op jit(solution)/shard_map/while
  384.3 7.6 %copy-start.9 = (bf16[1,1024,128]{2,1,0:T(8,128)(2,1)}, bf16[1,1024,128]{2,1,0:T(8,128)(2,1)S(1)}, u32[]{:S(2)}) copy-start(bf16[1,1024,128]{2,1,0:T(8,128)(2,1)S(1)} %get-tuple-element.520) | copy-start | bytes 786436 | tf_op jit(solution)/shard_map/while
  384.5 7.5 copy-start.3
  384.5 11.3 %copy-start = (bf16[1,1,5120,128]{3,2,1,0:T(8,128)(2,1)}, bf16[1,1,5120,128]{3,2,1,0:T(8,128)(2,1)S(1)}, u32[]{:S(2)}) copy-start(bf16[1,1,5120,128]{3,2,1,0:T(8,128)(2,1)S(1)} %get-tuple-element.518) | copy-start | bytes 3932164 | tf_op jit(solution)/shard_map/while
  409.4 11.4 %slice-start.2 = ((s8[4718592]{0:T(1024)(128)(4,1)}), s8[4194304]{0:T(1024)(128)(4,1)S(1)}, s32[]{:S(2)}) async-start(s8[4718592]{0:T(1024)(128)(4,1)} %bitcast.195), calls=%async_computation.7 | async-start | bytes 8388608 | tf_op jit(solution)/shard_map/while
  414.3 6.5 slice-start.3
  419.3 5.0 slice-start
  426.4 4.7 copy-start.2
  426.4 4.7 copy-start.6
  431.1 14.1 %copy-start.5 = (bf16[1024,384]{1,0:T(8,128)(2,1)}, bf16[1024,384]{1,0:T(8,128)(2,1)S(1)}, u32[]{:S(2)}) copy-start(bf16[1024,384]{1,0:T(8,128)(2,1)S(1)} %get-tuple-element.567) | copy-start | bytes 2359300 | tf_op jit(solution)/shard_map/while
  433.7 7.6 %copy-start.9 = (bf16[1,1024,128]{2,1,0:T(8,128)(2,1)}, bf16[1,1024,128]{2,1,0:T(8,128)(2,1)S(1)}, u32[]{:S(2)}) copy-start(bf16[1,1024,128]{2,1,0:T(8,128)(2,1)S(1)} %get-tuple-element.520) | copy-start | bytes 786436 | tf_op jit(solution)/shard_map/while
  433.9 7.5 copy-start.3
  433.9 11.3 %copy-start = (bf16[1,1,5120,128]{3,2,1,0:T(8,128)(2,1)}, bf16[1,1,5120,128]{3,2,1,0:T(8,128)(2,1)S(1)}, u32[]{:S(2)}) copy-start(bf16[1,1,5120,128]{3,2,1,0:T(8,128)(2,1)S(1)} %get-tuple-element.518) | copy-start | bytes 3932164 | tf_op jit(solution)/shard_map/while
  458.8 11.4 %slice-start.2 = ((s8[4718592]{0:T(1024)(128)(4,1)}), s8[4194304]{0:T(1024)(128)(4,1)S(1)}, s32[]{:S(2)}) async-start(s8[4718592]{0:T(1024)(128)(4,1)} %bitcast.195), calls=%async_computation.7 | async-start | bytes 8388608 | tf_op jit(solution)/shard_map/while
  463.8 6.5 slice-start.3
  468.8 5.0 slice-start
  484.7 41.3 %collective-permute-start.4 = (f32[2,1,1024,128]{3,2,1,0:T(8,128)}, f32[2,1,1024,128]{3,2,1,0:T(8,128)S(1)}, u32[]{:S(2)}, u32[]{:S(2)}) collective-permute-start(f32[2,1,1024,128]{3,2,1,0:T(8,128)} %get-tuple-element.420), channel_id=1, source_target_pairs={{8,0},{16,8},{24,16},{32,24},{40,32},{48,40},{56,48},{64,56},{72,6... | collective-permute-start | bytes 3145736 | tf_op jit(solution)/shard_map/ppermute | solution.py:13
  487.8 68.4 %collective-permute-start.5 = (f32[2,1,1024,128]{3,2,1,0:T(8,128)}, f32[2,1,1024,128]{3,2,1,0:T(8,128)}, u32[]{:S(2)}, u32[]{:S(2)}) collective-permute-start(f32[2,1,1024,128]{3,2,1,0:T(8,128)} %get-tuple-element.421), channel_id=1, source_target_pairs={{16,0},{24,8},{32,16},{40,24},{48,32},{56,40},{64,48},{72,56},{80,... | collective-permute-start | bytes 3145736 | tf_op jit(solution)/shard_map/ppermute | solution.py:13
  490.6 88.0 %collective-permute-start.7 = (f32[2,1,1024,128]{3,2,1,0:T(8,128)}, f32[2,1,1024,128]{3,2,1,0:T(8,128)}, u32[]{:S(2)}, u32[]{:S(2)}) collective-permute-start(f32[2,1,1024,128]{3,2,1,0:T(8,128)} %get-tuple-element.422), channel_id=1, source_target_pairs={{32,0},{40,8},{48,16},{56,24},{64,32},{72,40},{80,48},{88,56},{96,... | collective-permute-start | bytes 3145736 | tf_op jit(solution)/shard_map/ppermute | solution.py:13
  493.4 103.1 %collective-permute-start.6 = (f32[2,1,1024,128]{3,2,1,0:T(8,128)S(1)}, f32[2,1,1024,128]{3,2,1,0:T(8,128)}, u32[]{:S(2)}, u32[]{:S(2)}) collective-permute-start(f32[2,1,1024,128]{3,2,1,0:T(8,128)S(1)} %get-tuple-element.423), channel_id=1, source_target_pairs={{24,0},{32,8},{40,16},{48,24},{56,32},{64,40},{72,48},{80,56},{88,... | collective-permute-start | bytes 3145736 | tf_op jit(solution)/shard_map/ppermute | solution.py:13
  495.3 110.8 %all-to-all-start.1 = ((bf16[8,128,384]{2,1,0:T(8,128)(2,1)}), bf16[8,128,384]{2,1,0:T(8,128)(2,1)S(1)}, u32[]{:S(2)}, u32[]{:S(2)}) async-start(bf16[8,128,384]{2,1,0:T(8,128)(2,1)} %bitcast.12), calls=%async_computation.1 | async-start | bytes 1572864 | tf_op jit(solution)/shard_map/all_to_all | solution.py:144
  596.5 15.7 %copy-start.16 = (bf16[3,1024,128]{2,1,0:T(8,128)(2,1)S(1)}, bf16[3,1024,128]{2,1,0:T(8,128)(2,1)}, u32[]{:S(2)}) copy-start(bf16[3,1024,128]{2,1,0:T(8,128)(2,1)} %param.17) | copy-start | bytes 2359300
  606.1 17.9 %all-to-all-start.2 = ((bf16[8,128,128]{2,1,0:T(8,128)(2,1)}), bf16[8,128,128]{2,1,0:T(8,128)(2,1)S(1)}, u32[]{:S(2)}, u32[]{:S(2)}) async-start(bf16[8,128,128]{2,1,0:T(8,128)(2,1)} %bitcast.17), calls=%async_computation.2 | async-start | bytes 524288 | tf_op jit(solution)/shard_map/all_to_all | solution.py:145
  624.0 129.8 %all-to-all-start.3 = ((bf16[8,128,128]{2,1,0:T(8,128)(2,1)}), bf16[8,128,128]{2,1,0:T(8,128)(2,1)S(1)}, u32[]{:S(2)}, u32[]{:S(2)}) async-start(bf16[8,128,128]{2,1,0:T(8,128)(2,1)} %bitcast.20), calls=%async_computation.3 | async-start | bytes 524288 | tf_op jit(solution)/shard_map/all_to_all | solution.py:146
  (21 other events, 60.6 us)
Sparse Core Ops, SparseCore 0:
  192.9 167.9 all-gather.1
where the time goes:
time: 768 us; the launch traced here: 762 us
  waiting for transfers between devices  319 us (42%)
  matrix products  115 us (15%)
  blocking collectives  113 us (15%)
  local copies, waits for them, and re-layouts  97.2 us (13%)
  other arithmetic  51.5 us (7%)
  starting transfers between devices  50.8 us (7%)
  between operations  14.7 us (2%)
    ppermute x8, waiting for transfers between devices, shifted(): return lax.ppermute(block, axis, route)  142 us
    psum x1, blocking collectives, local(): summed_proj = lax.psum(partial_value, 'seq')  113 us
    all_gather x1, waiting for transfers between devices, local(): piece = lax.all_gather(hidden, 'head', axis=0, tiled=True)  103 us
    all_to_all x1, waiting for transfers between devices, local(): lax.all_to_all(expert_rows, 'head', split_axis=1, concat_axis=0, tiled=True)  67.1 us
    unnamed x31, local copies, waits for them, and re-layouts  55.6 us
    unnamed x1, other arithmetic  38.9 us
    dot_general x6, matrix products, block_step(): lax.dot_general(query_blk, key_blk, (((1,), (1,)), ((), ())), preferred_e...  25.6 us
    ppermute x8, starting transfers between devices, shifted(): return lax.ppermute(block, axis, route)  22.1 us
  transfers between devices with their start and end apart: 13, of which 11 were waited for; matrix products, arithmetic and copies ran while one was open for 4% of the time, Pallas kernels for 0%

commit v1 on v0

--- a/solution.py
+++ b/solution.py
@@ -43,7 +43,12 @@
     kv_dev = saved_keys.shape[0]
     group_size = heads_dev // kv_dev
     model_width = out_grad.shape[1]
-    returned = lax.all_to_all(expert_rows, "head", split_axis=1, concat_axis=0, tiled=True)
+    returned = jnp.concatenate(
+        lax.all_to_all(
+            jnp.stack(jnp.split(expert_rows, lax.axis_size("head"), axis=1)), "head", 0, 0
+        ),
+        axis=0,
+    )
     picked = routed_rows(returned, expert_ids)
     summed = out_grad.astype(jnp.float32)
     summed = summed + gates[:, 0:1] * picked[:, 0].astype(jnp.float32)

time: 768 us -> 722 us (0.940)
  other arithmetic: 51.5 us -> 12.4 us
  local copies, waits for them, and re-layouts: 97.2 us -> 69.3 us
  loops' own time: 0.85 us -> 18.6 us
    unnamed x1 -> x0, other arithmetic: 38.9 us -> none
    unnamed x31 -> x33, local copies, waits for them, and re-layouts: 55.6 us -> 26.1 us
    another operation x1, loops' own time: 0.85 us -> 18.6 us  [local(): lax.fori_loop(0, seq_dev // block_rows, block_step, loop_carry)]
  transfers between devices with their start and end apart: 13 -> 13, of which waited for: 11 -> 11; matrix products, arithmetic and copies ran while one was open for 4% -> 5% of each run, Pallas kernels for 0% -> 0%
where the time goes in v1:
time: 722 us; the launch traced here: 713 us
  waiting for transfers between devices  319 us (44%)
  matrix products  115 us (16%)
  blocking collectives  113 us (16%)
  local copies, waits for them, and re-layouts  69.3 us (10%)
  starting transfers between devices  51.2 us (7%)
  loops' own time  18.6 us (3%)
  between operations  14.7 us (2%)
  other arithmetic  12.4 us (2%)
    ppermute x8, waiting for transfers between devices, shifted(): return lax.ppermute(block, axis, route)  142 us
    psum x1, blocking collectives, local(): summed_proj = lax.psum(partial_value, 'seq')  113 us
    all_gather x1, waiting for transfers between devices, local(): piece = lax.all_gather(hidden, 'head', axis=0, tiled=True)  103 us
    all_to_all x1, waiting for transfers between devices, local(): lax.all_to_all(jnp.stack(jnp.split(expert_rows, lax.axis_size('head'), ax...  67.3 us
    unnamed x33, local copies, waits for them, and re-layouts  26.1 us
    dot_general x6, matrix products, block_step(): lax.dot_general(query_blk, key_blk, (((1,), (1,)), ((), ())), preferred_e...  25.6 us
    ppermute x8, starting transfers between devices, shifted(): return lax.ppermute(block, axis, route)  22.4 us
    dot_general x6, matrix products, block_step(): lax.dot_general(grad_blk, value_blk, (((1,), (1,)), ((), ())), preferred_...  20.5 us
  transfers between devices with their start and end apart: 13, of which 11 were waited for; matrix products, arithmetic and copies ran while one was open for 5% of the time, Pallas kernels for 0%

profile of v1, /device:TPU:6, one launch (start us, length us, event | category | flops | bytes accessed | tf_op | source)
XLA Modules:
  0.0 713.1 jit_solution(18419546368677947312)
XLA Ops:
  23.8 8.4 %all-to-all-start = ((bf16[8,1,64,6144]{3,2,1,0:T(8,128)(2,1)}), bf16[8,1,64,6144]{3,2,1,0:T(8,128)(2,1)}, u32[]{:S(2)}, u32[]{:S(2)}) async-start(bf16[8,1,64,6144]{3,2,1,0:T(8,128)(2,1)} %bitcast_dynamic-update-slice_fusion), calls=%async_computation | async-start | bytes 12582912 | tf_op jit(solution)/shard_map/all_to_all | solution.py:47
  35.7 67.3 %all-to-all-done = bf16[8,1,64,6144]{3,2,1,0:T(8,128)(2,1)} async-done(((bf16[8,1,64,6144]{3,2,1,0:T(8,128)(2,1)}), bf16[8,1,64,6144]{3,2,1,0:T(8,128)(2,1)}, u32[]{:S(2)}, u32[]{:S(2)}) %all-to-all-start) | async-done | bytes 6291488 | tf_op jit(solution)/shard_map/all_to_all | solution.py:47
  103.0 9.1 %gather_fusion = bf16[256,6144]{1,0:T(8,128)(2,1)S(1)} fusion(bf16[512,6144]{1,0:T(8,128)(2,1)} %bitcast.13, s32[1024]{0:T(1024)S(1)} %pad_clamp_fusion), kind=kCustom, calls=%fused_computation | custom fusion | bytes 6292480 | tf_op jit(solution)/shard_map/jit(_take)/gather | solution.py:26
  115.4 7.2 %copy.61 = bf16[128,2,6144]{0,2,1:T(8,128)(2,1)S(1)} copy(bf16[128,2,6144]{2,1,0:T(2,128)(2,1)} %gather.7) | data formatting | bytes 6291456 | tf_op jit(solution)/shard_map/jit(_take)/gather | solution.py:26
  126.9 5.1 collective-permute-start
  138.7 12.7 %collective-permute-done = bf16[2,1,1024,128]{3,2,1,0:T(8,128)(2,1)} collective-permute-done((bf16[2,1,1024,128]{3,2,1,0:T(8,128)(2,1)}, bf16[2,1,1024,128]{3,2,1,0:T(8,128)(2,1)}, u32[]{:S(2)}, u32[]{:S(2)}) %collective-permute-start) | collective-permute-done | bytes 524320 | tf_op jit(solution)/shard_map/ppermute | solution.py:13
  152.5 8.6 %collective-permute-done.1 = bf16[2,1,1024,128]{3,2,1,0:T(8,128)(2,1)} collective-permute-done((bf16[2,1,1024,128]{3,2,1,0:T(8,128)(2,1)}, bf16[2,1,1024,128]{3,2,1,0:T(8,128)(2,1)}, u32[]{:S(2)}, u32[]{:S(2)}) %collective-permute-start.1) | collective-permute-done | bytes 524320 | tf_op jit(solution)/shard_map/ppermute | solution.py:13
  162.2 24.2 %collective-permute-done.2 = bf16[2,1,1024,128]{3,2,1,0:T(8,128)(2,1)} collective-permute-done((bf16[2,1,1024,128]{3,2,1,0:T(8,128)(2,1)}, bf16[2,1,1024,128]{3,2,1,0:T(8,128)(2,1)}, u32[]{:S(2)}, u32[]{:S(2)}) %collective-permute-start.2) | collective-permute-done | bytes 524320 | tf_op jit(solution)/shard_map/ppermute | solution.py:13
  190.8 103.3 %all-gather.2.cloned.1.call-done = bf16[1024,6144]{0,1:T(8,128)(2,1)} async-done(((bf16[128,6144]{0,1:T(8,128)(2,1)}), bf16[1024,6144]{0,1:T(8,128)(2,1)}) %all-gather.2.cloned.1.call-update) | async-done | bytes 12582928 | tf_op jit(solution)/shard_map/all_gather | solution.py:57
  294.1 10.1 %convolution_convert_fusion = bf16[1024,384]{0,1:T(8,128)(2,1)} fusion(bf16[384,6144]{1,0:T(8,128)(2,1)} %param.16, bf16[1024,6144]{0,1:T(8,128)(2,1)} %all-gather.2.cloned.1.call-done), kind=kOutput, calls=%fused_computation.120 | convolution fusion | flops 4832231424 | bytes 18087936 | tf_op jit(solution)/shard_map/dot_general | solution.py:58
  314.7 116.9 %while.20 = (s32[]{:T(128)}, f32[1,5120,128]{2,1,0:T(8,128)}, f32[1,5120,128]{2,1,0:T(8,128)}, bf16[1024,384]{1,0:T(8,128)(2,1)}, s32[]{:T(128)}, /*index=5*/bf1...) while((s32[]{:T(128)}, f32[1,5120,128]{2,1,0:T(8,128)}, ...), condition=%wide.region_5.6_spmd.clone, body=%wide.region_4.5_spmd.clone.sunk | while | flops 9156034560 | bytes 252151056 | solution.py:136
  335.4 3.8 exponential_select_fusion.8
  342.9 3.8 exponential_select_fusion.7
  350.4 5.2 exponential_select_fusion.6
  360.3 4.9 fusion.204
  377.3 4.7 fusion.202
  392.3 3.8 exponential_select_fusion.7
  399.8 5.2 exponential_select_fusion.6
  409.7 4.9 fusion.204
  426.8 4.7 fusion.202
  431.7 3.9 fusion.109
  446.2 7.0 all-to-all-start.1
  453.2 23.5 %collective-permute-done.4 = f32[2,1,1024,128]{3,2,1,0:T(8,128)S(1)} collective-permute-done((f32[2,1,1024,128]{3,2,1,0:T(8,128)}, f32[2,1,1024,128]{3,2,1,0:T(8,128)S(1)}, u32[]{:S(2)}, u32[]{:S(2)}) %collective-permute-start.4) | collective-permute-done | bytes 1048608 | tf_op jit(solution)/shard_map/ppermute | solution.py:13
  476.7 30.3 %collective-permute-done.5 = f32[2,1,1024,128]{3,2,1,0:T(8,128)} collective-permute-done((f32[2,1,1024,128]{3,2,1,0:T(8,128)}, f32[2,1,1024,128]{3,2,1,0:T(8,128)}, u32[]{:S(2)}, u32[]{:S(2)}) %collective-permute-start.5) | collective-permute-done | bytes 1048608 | tf_op jit(solution)/shard_map/ppermute | solution.py:13
  507.1 22.5 %collective-permute-done.7 = f32[2,1,1024,128]{3,2,1,0:T(8,128)} collective-permute-done((f32[2,1,1024,128]{3,2,1,0:T(8,128)}, f32[2,1,1024,128]{3,2,1,0:T(8,128)}, u32[]{:S(2)}, u32[]{:S(2)}) %collective-permute-start.7) | collective-permute-done | bytes 1048608 | tf_op jit(solution)/shard_map/ppermute | solution.py:13
  529.5 17.9 %collective-permute-done.6 = f32[2,1,1024,128]{3,2,1,0:T(8,128)} collective-permute-done((f32[2,1,1024,128]{3,2,1,0:T(8,128)S(1)}, f32[2,1,1024,128]{3,2,1,0:T(8,128)}, u32[]{:S(2)}, u32[]{:S(2)}) %collective-permute-start.6) | collective-permute-done | bytes 1048608 | tf_op jit(solution)/shard_map/ppermute | solution.py:13
  550.7 6.4 all-to-all-done.1
  557.0 6.2 all-to-all-start.2
  563.2 11.8 %fusion.95 = f32[3,128,6144]{1,2,0:T(8,128)} fusion(bf16[3,1024,128]{2,1,0:T(8,128)(2,1)S(1)} %copy-done.16, bf16[1024,6144]{0,1:T(8,128)(2,1)} %all-gather.2.cloned.1.call-done), kind=kOutput, calls=%fused_computation.101 | convolution fusion | flops 4831838208 | bytes 22806528 | tf_op jit(solution)/shard_map/dot_general | solution.py:61
  575.0 7.2 %all-to-all-start.3 = ((bf16[8,128,128]{2,1,0:T(8,128)(2,1)}), bf16[8,128,128]{2,1,0:T(8,128)(2,1)S(1)}, u32[]{:S(2)}, u32[]{:S(2)}) async-start(bf16[8,128,128]{2,1,0:T(8,128)(2,1)} %bitcast.29), calls=%async_computation.3 | async-start | bytes 524288 | tf_op jit(solution)/shard_map/all_to_all | solution.py:151
  582.2 113.4 %all-reduce.1 = bf16[3,128,6144]{1,2,0:T(8,128)(2,1)} all-reduce(f32[3,128,6144]{1,2,0:T(8,128)} %fusion.95), channel_id=1, replica_groups=mesh['seq'=16,'head'=8] {'seq'}, use_global_device_ids=true, to_apply=%region_6.7 | all-reduce | flops 2359296 | bytes 14155776 | tf_op jit(solution)/shard_map/psum | solution.py:65
  695.6 6.6 copy.67
  (186 shorter events, 126.1 us)
Async XLA Ops:
  23.8 8.4 %copy-start.18 = (s32[128,2]{0,1:T(2,128)S(1)}, s32[128,2]{0,1:T(2,128)}, u32[]{:S(2)}) copy-start(s32[128,2]{0,1:T(2,128)} %param.14) | copy-start | bytes 3076
  23.8 10.2 %copy-start.13 = (bf16[128,6144]{1,0:T(8,128)(2,1)S(1)}, bf16[128,6144]{1,0:T(8,128)(2,1)}, u32[]{:S(2)}) copy-start(bf16[128,6144]{1,0:T(8,128)(2,1)} %param.12) | copy-start | bytes 4718596
  23.8 11.9 %copy-start.19 = (f32[128,2]{0,1:T(2,128)S(1)}, f32[128,2]{0,1:T(2,128)}, u32[]{:S(2)}) copy-start(f32[128,2]{0,1:T(2,128)} %param.15) | copy-start | bytes 3076
  23.8 79.2 %all-to-all-start = ((bf16[8,1,64,6144]{3,2,1,0:T(8,128)(2,1)}), bf16[8,1,64,6144]{3,2,1,0:T(8,128)(2,1)}, u32[]{:S(2)}, u32[]{:S(2)}) async-start(bf16[8,1,64,6144]{3,2,1,0:T(8,128)(2,1)} %bitcast_dynamic-update-slice_fusion), calls=%async_computation | async-start | bytes 12582912 | tf_op jit(solution)/shard_map/all_to_all | solution.py:47
  32.2 261.9 %all-gather.2.cloned.1.call-start = ((), (), s32[]{:S(2)}) async-start(), calls=%async_computation.4 | async-start | bytes 14155776 | tf_op jit(solution)/shard_map/all_gather | solution.py:57
  126.9 24.5 %collective-permute-start = (bf16[2,1,1024,128]{3,2,1,0:T(8,128)(2,1)}, bf16[2,1,1024,128]{3,2,1,0:T(8,128)(2,1)}, u32[]{:S(2)}, u32[]{:S(2)}) collective-permute-start(bf16[2,1,1024,128]{3,2,1,0:T(8,128)(2,1)} %pad_maximum_fusion.1), channel_id=1, source_target_pairs={{0,32},{8,40},{16,48},{24,56},{32,64},{40,72},{48,80},{56,88},{64,... | collective-permute-start | bytes 1572872 | tf_op jit(solution)/shard_map/ppermute | solution.py:13
  132.0 29.1 %collective-permute-start.1 = (bf16[2,1,1024,128]{3,2,1,0:T(8,128)(2,1)}, bf16[2,1,1024,128]{3,2,1,0:T(8,128)(2,1)}, u32[]{:S(2)}, u32[]{:S(2)}) collective-permute-start(bf16[2,1,1024,128]{3,2,1,0:T(8,128)(2,1)} %pad_maximum_fusion.1), channel_id=1, source_target_pairs={{0,24},{8,32},{16,40},{24,48},{32,56},{40,64},{48,72},{56,80},{64,... | collective-permute-start | bytes 1572872 | tf_op jit(solution)/shard_map/ppermute | solution.py:13
  133.9 52.5 %collective-permute-start.2 = (bf16[2,1,1024,128]{3,2,1,0:T(8,128)(2,1)}, bf16[2,1,1024,128]{3,2,1,0:T(8,128)(2,1)}, u32[]{:S(2)}, u32[]{:S(2)}) collective-permute-start(bf16[2,1,1024,128]{3,2,1,0:T(8,128)(2,1)} %pad_maximum_fusion.1), channel_id=1, source_target_pairs={{0,16},{8,24},{16,32},{24,40},{32,48},{40,56},{48,64},{56,72},{64,... | collective-permute-start | bytes 1572872 | tf_op jit(solution)/shard_map/ppermute | solution.py:13
  136.5 53.1 %collective-permute-start.3 = (bf16[2,1,1024,128]{3,2,1,0:T(8,128)(2,1)}, bf16[2,1,1024,128]{3,2,1,0:T(8,128)(2,1)}, u32[]{:S(2)}, u32[]{:S(2)}) collective-permute-start(bf16[2,1,1024,128]{3,2,1,0:T(8,128)(2,1)} %pad_maximum_fusion.1), channel_id=1, source_target_pairs={{0,8},{8,16},{16,24},{24,32},{32,40},{40,48},{48,56},{56,64},{64,7... | collective-permute-start | bytes 1572872 | tf_op jit(solution)/shard_map/ppermute | solution.py:13
  308.3 6.4 copy-start.17
  332.6 6.6 copy-start.1
  332.6 14.1 %copy-start.5 = (bf16[1024,384]{1,0:T(8,128)(2,1)}, bf16[1024,384]{1,0:T(8,128)(2,1)S(1)}, u32[]{:S(2)}) copy-start(bf16[1024,384]{1,0:T(8,128)(2,1)S(1)} %get-tuple-element.567) | copy-start | bytes 2359300 | tf_op jit(solution)/shard_map/while
  335.2 7.7 %copy-start.9 = (bf16[1,1024,128]{2,1,0:T(8,128)(2,1)}, bf16[1,1024,128]{2,1,0:T(8,128)(2,1)S(1)}, u32[]{:S(2)}) copy-start(bf16[1,1024,128]{2,1,0:T(8,128)(2,1)S(1)} %get-tuple-element.520) | copy-start | bytes 786436 | tf_op jit(solution)/shard_map/while
  335.4 7.5 %copy-start.3 = (bf16[1,1,5120,128]{3,2,1,0:T(8,128)(2,1)}, bf16[1,1,5120,128]{3,2,1,0:T(8,128)(2,1)S(1)}, u32[]{:S(2)}) copy-start(bf16[1,1,5120,128]{3,2,1,0:T(8,128)(2,1)S(1)} %get-tuple-element.515) | copy-start | bytes 3932164 | tf_op jit(solution)/shard_map/while
  335.4 11.3 %copy-start = (bf16[1,1,5120,128]{3,2,1,0:T(8,128)(2,1)}, bf16[1,1,5120,128]{3,2,1,0:T(8,128)(2,1)S(1)}, u32[]{:S(2)}) copy-start(bf16[1,1,5120,128]{3,2,1,0:T(8,128)(2,1)S(1)} %get-tuple-element.518) | copy-start | bytes 3932164 | tf_op jit(solution)/shard_map/while
  360.3 11.4 %slice-start.2 = ((s8[4718592]{0:T(1024)(128)(4,1)}), s8[4194304]{0:T(1024)(128)(4,1)S(1)}, s32[]{:S(2)}) async-start(s8[4718592]{0:T(1024)(128)(4,1)} %bitcast.205), calls=%async_computation.7 | async-start | bytes 8388608 | tf_op jit(solution)/shard_map/while
  365.2 6.5 slice-start.3
  382.1 6.6 copy-start.1
  382.1 14.1 %copy-start.5 = (bf16[1024,384]{1,0:T(8,128)(2,1)}, bf16[1024,384]{1,0:T(8,128)(2,1)S(1)}, u32[]{:S(2)}) copy-start(bf16[1024,384]{1,0:T(8,128)(2,1)S(1)} %get-tuple-element.567) | copy-start | bytes 2359300 | tf_op jit(solution)/shard_map/while
  384.7 7.6 %copy-start.9 = (bf16[1,1024,128]{2,1,0:T(8,128)(2,1)}, bf16[1,1024,128]{2,1,0:T(8,128)(2,1)S(1)}, u32[]{:S(2)}) copy-start(bf16[1,1024,128]{2,1,0:T(8,128)(2,1)S(1)} %get-tuple-element.520) | copy-start | bytes 786436 | tf_op jit(solution)/shard_map/while
  384.8 7.5 %copy-start.3 = (bf16[1,1,5120,128]{3,2,1,0:T(8,128)(2,1)}, bf16[1,1,5120,128]{3,2,1,0:T(8,128)(2,1)S(1)}, u32[]{:S(2)}) copy-start(bf16[1,1,5120,128]{3,2,1,0:T(8,128)(2,1)S(1)} %get-tuple-element.515) | copy-start | bytes 3932164 | tf_op jit(solution)/shard_map/while
  384.8 11.3 %copy-start = (bf16[1,1,5120,128]{3,2,1,0:T(8,128)(2,1)}, bf16[1,1,5120,128]{3,2,1,0:T(8,128)(2,1)S(1)}, u32[]{:S(2)}) copy-start(bf16[1,1,5120,128]{3,2,1,0:T(8,128)(2,1)S(1)} %get-tuple-element.518) | copy-start | bytes 3932164 | tf_op jit(solution)/shard_map/while
  409.7 11.4 %slice-start.2 = ((s8[4718592]{0:T(1024)(128)(4,1)}), s8[4194304]{0:T(1024)(128)(4,1)S(1)}, s32[]{:S(2)}) async-start(s8[4718592]{0:T(1024)(128)(4,1)} %bitcast.205), calls=%async_computation.7 | async-start | bytes 8388608 | tf_op jit(solution)/shard_map/while
  414.7 6.5 slice-start.3
  435.6 41.2 %collective-permute-start.4 = (f32[2,1,1024,128]{3,2,1,0:T(8,128)}, f32[2,1,1024,128]{3,2,1,0:T(8,128)S(1)}, u32[]{:S(2)}, u32[]{:S(2)}) collective-permute-start(f32[2,1,1024,128]{3,2,1,0:T(8,128)} %get-tuple-element.420), channel_id=1, source_target_pairs={{8,0},{16,8},{24,16},{32,24},{40,32},{48,40},{56,48},{64,56},{72,6... | collective-permute-start | bytes 3145736 | tf_op jit(solution)/shard_map/ppermute | solution.py:13
  438.6 68.4 %collective-permute-start.5 = (f32[2,1,1024,128]{3,2,1,0:T(8,128)}, f32[2,1,1024,128]{3,2,1,0:T(8,128)}, u32[]{:S(2)}, u32[]{:S(2)}) collective-permute-start(f32[2,1,1024,128]{3,2,1,0:T(8,128)} %get-tuple-element.421), channel_id=1, source_target_pairs={{16,0},{24,8},{32,16},{40,24},{48,32},{56,40},{64,48},{72,56},{80,... | collective-permute-start | bytes 3145736 | tf_op jit(solution)/shard_map/ppermute | solution.py:13
  441.5 88.0 %collective-permute-start.7 = (f32[2,1,1024,128]{3,2,1,0:T(8,128)}, f32[2,1,1024,128]{3,2,1,0:T(8,128)}, u32[]{:S(2)}, u32[]{:S(2)}) collective-permute-start(f32[2,1,1024,128]{3,2,1,0:T(8,128)} %get-tuple-element.422), channel_id=1, source_target_pairs={{32,0},{40,8},{48,16},{56,24},{64,32},{72,40},{80,48},{88,56},{96,... | collective-permute-start | bytes 3145736 | tf_op jit(solution)/shard_map/ppermute | solution.py:13
  444.2 103.1 %collective-permute-start.6 = (f32[2,1,1024,128]{3,2,1,0:T(8,128)S(1)}, f32[2,1,1024,128]{3,2,1,0:T(8,128)}, u32[]{:S(2)}, u32[]{:S(2)}) collective-permute-start(f32[2,1,1024,128]{3,2,1,0:T(8,128)S(1)} %get-tuple-element.423), channel_id=1, source_target_pairs={{24,0},{32,8},{40,16},{48,24},{56,32},{64,40},{72,48},{80,56},{88,... | collective-permute-start | bytes 3145736 | tf_op jit(solution)/shard_map/ppermute | solution.py:13
  446.2 110.9 %all-to-all-start.1 = ((bf16[8,128,384]{2,1,0:T(8,128)(2,1)}), bf16[8,128,384]{2,1,0:T(8,128)(2,1)S(1)}, u32[]{:S(2)}, u32[]{:S(2)}) async-start(bf16[8,128,384]{2,1,0:T(8,128)(2,1)} %bitcast.21), calls=%async_computation.1 | async-start | bytes 1572864 | tf_op jit(solution)/shard_map/all_to_all | solution.py:149
  547.4 15.8 %copy-start.16 = (bf16[3,1024,128]{2,1,0:T(8,128)(2,1)S(1)}, bf16[3,1024,128]{2,1,0:T(8,128)(2,1)}, u32[]{:S(2)}) copy-start(bf16[3,1024,128]{2,1,0:T(8,128)(2,1)} %param.17) | copy-start | bytes 2359300
  557.0 18.0 %all-to-all-start.2 = ((bf16[8,128,128]{2,1,0:T(8,128)(2,1)}), bf16[8,128,128]{2,1,0:T(8,128)(2,1)S(1)}, u32[]{:S(2)}, u32[]{:S(2)}) async-start(bf16[8,128,128]{2,1,0:T(8,128)(2,1)} %bitcast.26), calls=%async_computation.2 | async-start | bytes 524288 | tf_op jit(solution)/shard_map/all_to_all | solution.py:150
  575.0 129.8 %all-to-all-start.3 = ((bf16[8,128,128]{2,1,0:T(8,128)(2,1)}), bf16[8,128,128]{2,1,0:T(8,128)(2,1)S(1)}, u32[]{:S(2)}, u32[]{:S(2)}) async-start(bf16[8,128,128]{2,1,0:T(8,128)(2,1)} %bitcast.29), calls=%async_computation.3 | async-start | bytes 524288 | tf_op jit(solution)/shard_map/all_to_all | solution.py:151
  (21 other events, 72.8 us)
Sparse Core Ops, SparseCore 0:
  126.1 167.9 all-gather.1
